TPU v7x, 32 devices: a whole 2x2x4 slice. The times are simulated.
32 devices in a mesh: tm: 4 (over y, x), tp: 8 (over z, core).
Axes of the slice: x: 2, y: 2, z: 4, core: 2. Of those that a mesh axis runs over, the one named last changes fastest.
Arguments:
- pixels: bfloat16 [8, 32, 32, 1176], P('tm', 'tp'), may hold values from -6 to 6
- conv_weight: bfloat16 [1176, 1280], P(None, 'tm'), may hold values from -0.1875 to 0.1875
- norm_gain: float32 [1280], replicated, may hold values from 0.1 to 1.9
- norm_bias: float32 [1280], replicated, may hold values from -3 to 3
- proj_in: bfloat16 [5120, 5120], P(None, 'tp'), may hold values from -0.078125 to 0.078125
- bias_in: float32 [5120], P('tp'), may hold values from -3 to 3
- proj_out: bfloat16 [5120, 8192], P(None, 'tp'), may hold values from -0.078125 to 0.078125
- bias_out: float32 [8192], P('tp'), may hold values from -3 to 3
Outputs:
- tokens_out: bfloat16 [8, 16, 16, 8192], P('tm', None, None, 'tp')
All inputs are finite; a program needn't handle non-finite values.
Results may differ from a plain program's by a relative error of at most 0.0052.
Values may be sent and summed in bfloat16 or wider, within the bound.
A program may use at most 64 MiB of HBM per device.

v0:
```python
import jax
import jax.numpy as jnp
from jax import lax
from jax.sharding import PartitionSpec as P


def per_device(pixels, conv_weight, norm_gain, norm_bias, proj_in, bias_in, proj_out, bias_out):
    kernel = lax.all_gather(conv_weight, "tm", axis=1, tiled=True)
    pairs_here, rows_here, cols_all, patch_len = pixels.shape
    channels = kernel.shape[1]
    embed = jnp.dot(pixels.reshape(-1, patch_len), kernel, preferred_element_type=jnp.float32)
    mean = jnp.mean(embed, axis=-1, keepdims=True)
    centred = embed - mean
    variance = jnp.mean(centred * centred, axis=-1, keepdims=True)
    normed = (centred * lax.rsqrt(variance + 1e-06) * norm_gain + norm_bias).astype(jnp.bfloat16)
    normed = normed.reshape(pairs_here, rows_here, cols_all, channels)
    items = normed.reshape(pairs_here, rows_here, cols_all // 2, 2, channels)
    items = items.transpose(0, 2, 1, 3, 4).reshape(
        pairs_here * (cols_all // 2), rows_here, 2, channels
    )
    moved = lax.all_to_all(items, "tp", split_axis=0, concat_axis=1, tiled=True)
    owned = moved.shape[0]
    rows_full = moved.shape[1]
    merged = moved.reshape(owned, rows_full // 2, 2, 2, channels).reshape(
        owned * (rows_full // 2), 4 * channels
    )
    pre = (
        jnp.dot(
            lax.all_gather(merged, "tp", axis=0, tiled=True),
            proj_in,
            preferred_element_type=jnp.float32,
        )
        + bias_in
    )
    hidden = jax.nn.gelu(pre, approximate=False).astype(jnp.bfloat16)
    out_cols = proj_out.shape[1]
    summed = jnp.dot(
        lax.all_gather(hidden, "tp", axis=1, tiled=True),
        proj_out,
        preferred_element_type=jnp.float32,
    )
    result = (summed + bias_out).astype(jnp.bfloat16)
    result = result.reshape(pairs_here, cols_all // 2, rows_full // 2, out_cols).transpose(
        0, 2, 1, 3
    )
    return result


def solution(mesh):
    return jax.shard_map(
        per_device,
        mesh=mesh,
        in_specs=(
            P("tm", "tp", None, None),
            P(None, "tm"),
            P(),
            P(),
            P(None, "tp"),
            P("tp"),
            P(None, "tp"),
            P("tp"),
        ),
        out_specs=P("tm", None, None, "tp"),
        check_vma=False,
    )
```

profile of v0, /device:TPU:0, one launch (start us, length us, event | category | flops | bytes accessed | tf_op | source)
XLA Modules:
  0.0 225.5 jit_solution(2503487744257658268)
XLA Ops:
  6.5 0.7 all-gather.4.cloned.1.call-update
  7.3 0.0 all-gather.6.cloned.1.call-start
  7.3 49.7 %all-gather.4.cloned.1.call-done = bf16[1176,1280]{0,1:T(8,128)(2,1)} async-done(((bf16[1176,320]{0,1:T(8,128)(2,1)}), bf16[1176,1280]{0,1:T(8,128)(2,1)}) %all-gather.4.cloned.1.call-update) | async-done | bytes 3010576 | tf_op jit(solution)/shard_map/all_gather | solution.py:8
  57.0 3.1 %fusion.10 = (f32[256]{0:T(256)S(1)}, f32[256,1280]{1,0:T(8,128)S(1)}) fusion(bf16[256,1176]{1,0:T(8,128)(2,1)S(1)} %bitcast.18, bf16[1176,1280]{0,1:T(8,128)(2,1)} %all-gather.4.cloned.1.call-done), kind=kOutput, calls=%fused_computation.27 | convolution fusion | flops 771030784 | bytes 4924416 | tf_op jit(solution)/shard_map/dot_general | solution.py:11
  60.1 0.0 copy-start.2
  60.1 0.3 multiply_reduce_fusion
  60.4 0.4 copy-done.1
  60.8 0.0 copy-done.2
  60.8 0.3 add_convert_fusion.1
  61.1 0.2 reshape_reshape.6
  61.4 0.1 copy.13
  61.4 0.7 copy.14
  62.1 22.6 %all_to_all.15 = bf16[32,4,2,1280]{3,2,1,0:T(2,128)(2,1)S(1)} all-to-all(bf16[32,4,2,1280]{3,2,1,0:T(2,128)(2,1)S(1)} %copy.14), channel_id=1, replica_groups=mesh['tm'=4,'tp'=8] {'tp'}, dimensions={0} | all-to-all | bytes 1310720 | tf_op jit(solution)/shard_map/all_to_all | solution.py:21
  84.7 0.5 copy.20
  85.1 0.0 copy-start.3
  85.2 1.3 reshape_reshape.7
  86.5 0.0 all-gather.6.cloned.1.call-update
  86.5 0.2 all-gather.8.cloned.1.call-start
  86.7 53.9 %all-gather.6.cloned.1.call-done = bf16[512,5120]{1,0:T(8,128)(2,1)} async-done(((bf16[64,5120]{1,0:T(8,128)(2,1)}), bf16[512,5120]{1,0:T(8,128)(2,1)}) %all-gather.6.cloned.1.call-update) | async-done | bytes 5242896 | tf_op jit(solution)/shard_map/all_gather | solution.py:29
  140.6 12.1 %fusion.2 = bf16[512,640]{1,0:T(8,128)(2,1)} fusion(bf16[512,5120]{1,0:T(8,128)(2,1)} %all-gather.6.cloned.1.call-done, bf16[5120,640]{1,0:T(8,128)(2,1)} %param.12, f32[640]{0:T(1024)S(1)} %copy-done.3), kind=kOutput, calls=%fused_computation.5 | convolution fusion | flops 3377070080 | bytes 12454400 | tf_op jit(solution)/shard_map/dot_general | solution.py:28
  152.7 0.0 all-gather.8.cloned.1.call-update
  152.8 54.8 %all-gather.8.cloned.1.call-done = bf16[512,5120]{1,0:T(8,128)(2,1)} async-done(((bf16[512,640]{1,0:T(8,128)(2,1)}), bf16[512,5120]{1,0:T(8,128)(2,1)}) %all-gather.8.cloned.1.call-update) | async-done | bytes 5242896 | tf_op jit(solution)/shard_map/all_gather | solution.py:38
  207.6 9.8 %add_convert_fusion = bf16[512,1024]{1,0:T(8,128)(2,1)S(1)} fusion(bf16[512,5120]{1,0:T(8,128)(2,1)} %all-gather.8.cloned.1.call-done, bf16[5120,1024]{1,0:T(8,128)(2,1)} %param.14, f32[1024]{0:T(1024)S(1)} %copy-done.4), kind=kOutput, calls=%fused_computation | convolution fusion | flops 5369757696 | bytes 16781312 | tf_op jit(solution)/shard_map/dot_general | solution.py:37
  217.4 1.5 copy.19
  (9 shorter events, 0.0 us)
Async XLA Ops:
  6.5 50.5 %copy-start = (bf16[2,4,32,1176]{3,2,1,0:T(8,128)(2,1)S(1)}, bf16[2,4,32,1176]{3,2,1,0:T(8,128)(2,1)}, u32[]{:S(2)}) copy-start(bf16[2,4,32,1176]{3,2,1,0:T(8,128)(2,1)} %param.8) | copy-start | bytes 1806340
  6.5 50.5 %all-gather.4.cloned.1.call-start = ((), (), s32[]{:S(2)}) async-start(), calls=%async_computation.1 | async-start | bytes 4096000 | tf_op jit(solution)/shard_map/all_gather | solution.py:8
  7.3 133.4 %all-gather.6.cloned.1.call-start = ((), (), s32[]{:S(2)}) async-start(), calls=%async_computation.2 | async-start | bytes 5898240 | tf_op jit(solution)/shard_map/all_gather | solution.py:29
  60.1 0.7 copy-start.1
  60.1 0.7 copy-start.2
  85.1 55.5 %copy-start.3 = (f32[640]{0:T(1024)S(1)}, f32[640]{0:T(1024)}, u32[]{:S(2)}) copy-start(f32[640]{0:T(1024)} %param.13) | copy-start | bytes 7684
  86.5 121.1 %copy-start.4 = (f32[1024]{0:T(1024)S(1)}, f32[1024]{0:T(1024)}, u32[]{:S(2)}) copy-start(f32[1024]{0:T(1024)} %param.15) | copy-start | bytes 12292
  86.5 121.1 %all-gather.8.cloned.1.call-start = ((), (), s32[]{:S(2)}) async-start(), calls=%async_computation.3 | async-start | bytes 5898240 | tf_op jit(solution)/shard_map/all_gather | solution.py:38
Sparse Core Ops, SparseCore 0:
  9.2 47.7 all-gather.3
  86.6 53.9 all-gather.5
  152.9 54.6 all-gather.7
where the time goes:
time: 226 us; the launch traced here: 225 us
  waiting for transfers between devices  159 us (70%)
  matrix products  25 us (11%)
  blocking collectives  22.6 us (10%)
  between operations  13.2 us (6%)
  local copies, waits for them, and re-layouts  4.74 us (2%)
    all_gather x1, waiting for transfers between devices, per_device(): lax.all_gather(hidden, 'tp', axis=1, tiled=True)  54.8 us
    all_gather x1, waiting for transfers between devices, per_device(): lax.all_gather(merged, 'tp', axis=0, tiled=True)  53.9 us
    all_gather x1, waiting for transfers between devices, per_device(): kernel = lax.all_gather(conv_weight, 'tm', axis=1, tiled=True)  49.7 us
    all_to_all x1, blocking collectives, per_device(): moved = lax.all_to_all(items, 'tp', split_axis=0, concat_axis=1, tiled=True)  22.6 us
    dot_general x1, matrix products, per_device(): jnp.dot(lax.all_gather(merged, 'tp', axis=0, tiled=True), proj_in, prefer...  12.1 us
    dot_general x1, matrix products, per_device(): jnp.dot(lax.all_gather(hidden, 'tp', axis=1, tiled=True), proj_out, prefe...  9.81 us
  transfers between devices with their start and end apart: 3, of which 3 were waited for; matrix products, arithmetic and copies ran while one was open for 0% of the time, Pallas kernels for 0%

commit v1 on v0

--- a/solution.py
+++ b/solution.py
@@ -4,7 +4,7 @@
 from jax.sharding import PartitionSpec as P
 
 
-def per_device(pixels, conv_weight, norm_gain, norm_bias, proj_in, bias_in, proj_out, bias_out):
+def per_device_split_blocks(pixels, conv_weight, norm_gain, norm_bias, proj_in, bias_in, proj_out, bias_out):
     kernel = lax.all_gather(conv_weight, "tm", axis=1, tiled=True)
     pairs_here, rows_here, cols_all, patch_len = pixels.shape
     channels = kernel.shape[1]
@@ -46,6 +46,47 @@
     return result
 
 
+def per_device_whole_blocks(pixels, conv_weight, norm_gain, norm_bias, proj_in, bias_in, proj_out, bias_out):
+    kernel = lax.all_gather(conv_weight, "tm", axis=1, tiled=True)
+    pairs_here, rows_here, cols_all, patch_len = pixels.shape
+    channels = kernel.shape[1]
+    embed = jnp.dot(pixels.reshape(-1, patch_len), kernel, preferred_element_type=jnp.float32)
+    mean = jnp.mean(embed, axis=-1, keepdims=True)
+    centred = embed - mean
+    variance = jnp.mean(centred * centred, axis=-1, keepdims=True)
+    normed = (centred * lax.rsqrt(variance + 1e-06) * norm_gain + norm_bias).astype(jnp.bfloat16)
+    normed = normed.reshape(pairs_here, rows_here, cols_all, channels)
+    merged = normed.reshape(pairs_here, rows_here // 2, 2, cols_all // 2, 2, channels)
+    merged = merged.transpose(0, 1, 3, 2, 4, 5).reshape(-1, 4 * channels)
+    pre = (
+        jnp.dot(
+            lax.all_gather(merged, "tp", axis=0, tiled=True),
+            proj_in,
+            preferred_element_type=jnp.float32,
+        )
+        + bias_in
+    )
+    hidden = jax.nn.gelu(pre, approximate=False).astype(jnp.bfloat16)
+    out_cols = proj_out.shape[1]
+    summed = jnp.dot(
+        lax.all_gather(hidden, "tp", axis=1, tiled=True),
+        proj_out,
+        preferred_element_type=jnp.float32,
+    )
+    result = (summed + bias_out).astype(jnp.bfloat16)
+    tp = lax.axis_size("tp")
+    result = result.reshape(tp, pairs_here, rows_here // 2, cols_all // 2, out_cols)
+    result = result.transpose(1, 0, 2, 3, 4).reshape(
+        pairs_here, tp * (rows_here // 2), cols_all // 2, out_cols
+    )
+    return result
+
+
+def per_device(pixels, *rest):
+    body = per_device_whole_blocks if pixels.shape[1] % 2 == 0 else per_device_split_blocks
+    return body(pixels, *rest)
+
+
 def solution(mesh):
     return jax.shard_map(
         per_device,

time: 226 us -> 204 us (0.903)
  blocking collectives: 22.6 us -> 0 us
    all_to_all x1 -> x0, blocking collectives: 22.6 us -> none  [per_device(): moved = lax.all_to_all(items, 'tp', split_axis=0, concat_axis=1, tiled=True)]
    all_gather x3, waiting for transfers between devices: 158 us -> 161 us  [the longest x1 56.1 us: per_device_whole_blocks(): lax.all_gather(merged, 'tp', axis=0, tiled=True)]
where the time goes in v1:
time: 204 us
  waiting for transfers between devices  161 us (79%)
  matrix products  25 us (12%)
  between operations  13.2 us (6%)
  local copies, waits for them, and re-layouts  3.5 us (2%)
    all_gather x1, waiting for transfers between devices, per_device_whole_blocks(): lax.all_gather(merged, 'tp', axis=0, tiled=True)  56.1 us
    all_gather x1, waiting for transfers between devices, per_device_whole_blocks(): lax.all_gather(hidden, 'tp', axis=1, tiled=True)  54.8 us
    all_gather x1, waiting for transfers between devices, per_device_whole_blocks(): kernel = lax.all_gather(conv_weight, 'tm', axis=1, tiled=True)  49.7 us
    dot_general x1, matrix products, per_device_whole_blocks(): jnp.dot(lax.all_gather(merged, 'tp', axis=0, tiled=True), proj_in, prefer...  12.1 us
    dot_general x1, matrix products, per_device_whole_blocks(): jnp.dot(lax.all_gather(hidden, 'tp', axis=1, tiled=True), proj_out, prefe...  9.81 us
  transfers between devices with their start and end apart: 3, of which 3 were waited for; matrix products, arithmetic and copies ran while one was open for 0% of the time, Pallas kernels for 0%

profile of v1, /device:TPU:0, one launch (start us, length us, event | category | flops | bytes accessed | tf_op | source)
XLA Modules:
  0.0 203.7 jit_solution(8500269029109640755)
XLA Ops:
  6.5 0.0 copy-start
  6.5 0.7 all-gather.4.cloned.1.call-update
  7.3 0.0 all-gather.6.cloned.1.call-start
  7.3 49.7 %all-gather.4.cloned.1.call-done = bf16[1176,1280]{0,1:T(8,128)(2,1)} async-done(((bf16[1176,320]{0,1:T(8,128)(2,1)}), bf16[1176,1280]{0,1:T(8,128)(2,1)}) %all-gather.4.cloned.1.call-update) | async-done | bytes 3010576 | tf_op jit(solution)/shard_map/all_gather | solution.py:50
  57.0 3.1 %fusion.10 = (f32[256]{0:T(256)S(1)}, f32[256,1280]{1,0:T(8,128)S(1)}) fusion(bf16[256,1176]{1,0:T(8,128)(2,1)S(1)} %bitcast.14, bf16[1176,1280]{0,1:T(8,128)(2,1)} %all-gather.4.cloned.1.call-done), kind=kOutput, calls=%fused_computation.26 | convolution fusion | flops 771030784 | bytes 4924416 | tf_op jit(solution)/shard_map/dot_general | solution.py:53
  60.1 0.0 copy-start.1
  60.1 0.0 copy-start.2
  60.1 0.3 multiply_reduce_fusion
  60.4 0.4 copy-done.1
  60.8 0.0 copy-done.2
  60.8 0.3 add_convert_fusion.1
  61.1 0.2 reshape_reshape.3
  61.4 0.5 copy.13
  61.8 0.0 copy-start.3
  61.8 1.3 reshape.29
  63.2 0.0 all-gather.6.cloned.1.call-update
  63.2 0.0 copy-start.4
  63.2 0.0 all-gather.8.cloned.1.call-start
  63.2 56.1 %all-gather.6.cloned.1.call-done = bf16[512,5120]{1,0:T(8,128)(2,1)} async-done(((bf16[64,5120]{1,0:T(8,128)(2,1)}), bf16[512,5120]{1,0:T(8,128)(2,1)}) %all-gather.6.cloned.1.call-update) | async-done | bytes 5242896 | tf_op jit(solution)/shard_map/all_gather | solution.py:63
  119.4 12.1 %fusion.2 = bf16[512,640]{1,0:T(8,128)(2,1)} fusion(bf16[512,5120]{1,0:T(8,128)(2,1)} %all-gather.6.cloned.1.call-done, bf16[5120,640]{1,0:T(8,128)(2,1)} %param.12, f32[640]{0:T(1024)S(1)} %copy-done.3), kind=kOutput, calls=%fused_computation.5 | convolution fusion | flops 3377070080 | bytes 12454400 | tf_op jit(solution)/shard_map/dot_general | solution.py:62
  131.5 0.0 all-gather.8.cloned.1.call-update
  131.5 54.8 %all-gather.8.cloned.1.call-done = bf16[512,5120]{1,0:T(8,128)(2,1)} async-done(((bf16[512,640]{1,0:T(8,128)(2,1)}), bf16[512,5120]{1,0:T(8,128)(2,1)}) %all-gather.8.cloned.1.call-update) | async-done | bytes 5242896 | tf_op jit(solution)/shard_map/all_gather | solution.py:72
  186.3 9.8 %add_convert_fusion = bf16[512,1024]{1,0:T(8,128)(2,1)S(1)} fusion(bf16[512,5120]{1,0:T(8,128)(2,1)} %all-gather.8.cloned.1.call-done, bf16[5120,1024]{1,0:T(8,128)(2,1)} %param.14, f32[1024]{0:T(1024)S(1)} %copy-done.4), kind=kOutput, calls=%fused_computation | convolution fusion | flops 5369757696 | bytes 16781312 | tf_op jit(solution)/shard_map/dot_general | solution.py:71
  196.1 1.0 copy.11
  (6 shorter events, 0.0 us)
Async XLA Ops:
  6.5 50.5 %copy-start = (bf16[2,4,32,1176]{3,2,1,0:T(8,128)(2,1)S(1)}, bf16[2,4,32,1176]{3,2,1,0:T(8,128)(2,1)}, u32[]{:S(2)}) copy-start(bf16[2,4,32,1176]{3,2,1,0:T(8,128)(2,1)} %param.8) | copy-start | bytes 1806340
  6.5 50.5 %all-gather.4.cloned.1.call-start = ((), (), s32[]{:S(2)}) async-start(), calls=%async_computation | async-start | bytes 4096000 | tf_op jit(solution)/shard_map/all_gather | solution.py:50
  7.3 112.1 %all-gather.6.cloned.1.call-start = ((), (), s32[]{:S(2)}) async-start(), calls=%async_computation.1 | async-start | bytes 5898240 | tf_op jit(solution)/shard_map/all_gather | solution.py:63
  60.1 0.7 copy-start.1
  60.1 0.7 copy-start.2
  61.8 57.6 %copy-start.3 = (f32[640]{0:T(1024)S(1)}, f32[640]{0:T(1024)}, u32[]{:S(2)}) copy-start(f32[640]{0:T(1024)} %param.13) | copy-start | bytes 7684
  63.2 123.1 %copy-start.4 = (f32[1024]{0:T(1024)S(1)}, f32[1024]{0:T(1024)}, u32[]{:S(2)}) copy-start(f32[1024]{0:T(1024)} %param.15) | copy-start | bytes 12292
  63.2 123.1 %all-gather.8.cloned.1.call-start = ((), (), s32[]{:S(2)}) async-start(), calls=%async_computation.2 | async-start | bytes 5898240 | tf_op jit(solution)/shard_map/all_gather | solution.py:72
Sparse Core Ops, SparseCore 0:
  9.2 47.7 all-gather.3
  63.3 56.0 all-gather.5
  131.6 54.6 all-gather.7

commit v2 on v1

--- a/solution.py
+++ b/solution.py
@@ -1,6 +1,10 @@
+import functools
+
 import jax
 import jax.numpy as jnp
 from jax import lax
+from jax.experimental import pallas as pl
+from jax.experimental.pallas import tpu as pltpu
 from jax.sharding import PartitionSpec as P
 
 
@@ -82,9 +86,353 @@
     return result
 
 
-def per_device(pixels, *rest):
-    body = per_device_whole_blocks if pixels.shape[1] % 2 == 0 else per_device_split_blocks
-    return body(pixels, *rest)
+MESH = pl.DeviceIdType.MESH
+EPS = 1e-06
+VMEM_BYTES = 60 * 1024 * 1024
+
+
+def fused_kernel(
+    dims,
+    x_ref, wide_ref, narrow_ref, gain_ref, shift_ref, bias_in_ref, bias_out_ref, proj_in_ref, proj_out_ref,
+    out_ref,
+    xs, kernel, narrow, lhs, embed, merged, hidden, win, wout,
+    own_sems, win_sems, wout_sem,
+    conv_send, conv_recv, conv_fwd_send, conv_fwd_recv,
+    x_send, x_recv, m_send, m_recv,
+    h_send, h_recv, h_own_send, h_own_recv, h_fwd_send, h_fwd_recv,
+):
+    tm_n, tp_n, pairs, bands, cols, main, rem, channels = dims
+    line_n = tp_n // 2
+    blocks = pairs * bands
+    line_rows = line_n * cols
+    hid_local = proj_in_ref.shape[1]
+    wide = wide_ref.shape[1]
+    thin = channels // tm_n - wide
+    half_wide = wide_ref.shape[0] // 2
+    half_narrow = narrow_ref.shape[0] // 2
+    tm = lax.axis_index("tm")
+    tp = lax.axis_index("tp")
+    core = lax.rem(tp, 2)
+    z = tp // 2
+    sibling = (tm, z * 2 + 1 - core)
+
+    def along_line(d):
+        return (tm, lax.rem(z + d, line_n) * 2 + core)
+
+    def along_tm(d):
+        return (lax.rem(tm + d, tm_n), tp)
+
+    def remote(src, dst, send, recv, device):
+        return pltpu.make_async_remote_copy(
+            src_ref=src, dst_ref=dst, send_sem=send, recv_sem=recv, device_id=device, device_id_type=MESH
+        )
+
+    barrier = pltpu.get_barrier_semaphore()
+    peers = [sibling]
+    peers += [along_line(d) for d in range(1, line_n)]
+    peers += [along_tm(d) for d in range(1, tm_n)]
+    for peer in peers:
+        pl.semaphore_signal(barrier, inc=1, device_id=peer, device_id_type=MESH)
+
+    own = [
+        pltpu.make_async_copy(wide_ref, kernel.at[:, pl.ds(pl.multiple_of(tm * wide, wide), wide)], own_sems.at[0]),
+        pltpu.make_async_copy(narrow_ref, narrow.at[tm], own_sems.at[1]),
+    ]
+    for s in range(blocks):
+        own.append(
+            pltpu.make_async_copy(
+                x_ref.at[pl.ds(s * cols, cols)],
+                xs.at[s, pl.ds(pl.multiple_of(z * cols, cols), cols)],
+                own_sems.at[2 + s],
+            )
+        )
+    weights = []
+    for q in range(4):
+        for t in range(tm_n):
+            first = q * channels + t * (wide + thin)
+            for src, dst, count in (
+                (first, q * channels + t * wide, wide),
+                (first + wide, q * channels + tm_n * wide + t * thin, thin),
+            ):
+                weights.append(
+                    pltpu.make_async_copy(
+                        proj_in_ref.at[pl.ds(src, count)], win.at[pl.ds(dst, count)], win_sems.at[len(weights)]
+                    )
+                )
+    weights_out = pltpu.make_async_copy(proj_out_ref, wout, wout_sem.at[0])
+    for copy in own + weights + [weights_out]:
+        copy.start()
+
+    pl.semaphore_wait(barrier, len(peers))
+
+    def wide_part(owner, half):
+        return kernel.at[
+            pl.ds(pl.multiple_of(half * half_wide, 16), half_wide),
+            pl.ds(pl.multiple_of(owner * wide, wide), wide),
+        ]
+
+    def narrow_part(owner, half):
+        return narrow.at[owner, pl.ds(pl.multiple_of(half * half_narrow, 16), half_narrow)]
+
+    conv = []
+    for d in range(1, tm_n):
+        i = 2 * (d - 1)
+        conv.append(
+            remote(
+                wide_ref.at[pl.ds(pl.multiple_of(core * half_wide, 16), half_wide)],
+                wide_part(tm, core), conv_send.at[i], conv_recv.at[i], along_tm(d),
+            )
+        )
+        conv.append(
+            remote(
+                narrow_ref.at[pl.ds(pl.multiple_of(core * half_narrow, 16), half_narrow)],
+                narrow_part(tm, core), conv_send.at[i + 1], conv_recv.at[i + 1], along_tm(d),
+            )
+        )
+    for copy in conv:
+        copy.start()
+
+    def x_part(s, place):
+        return xs.at[s, pl.ds(pl.multiple_of(place * cols, cols), cols)]
+
+    pixels = []
+    for s in range(blocks):
+        for d in range(1, line_n):
+            pixels.append(
+                remote(
+                    x_ref.at[pl.ds(s * cols, cols)], x_part(s, z),
+                    x_send.at[s, d - 1], x_recv.at[s, d - 1], along_line(d),
+                )
+            )
+    for copy in pixels:
+        copy.start()
+
+    forwards = []
+    for d in range(1, tm_n):
+        i = 2 * (d - 1)
+        owner = lax.rem(tm - d + tm_n, tm_n)
+        for k, part in ((i, wide_part(owner, core)), (i + 1, narrow_part(owner, core))):
+            remote(part, part, conv_send.at[k], conv_recv.at[k], sibling).wait_recv()
+            copy = remote(part, part, conv_fwd_send.at[k], conv_fwd_recv.at[k], sibling)
+            copy.start()
+            forwards.append(copy)
+    for copy in own:
+        copy.wait()
+    for d in range(1, tm_n):
+        i = 2 * (d - 1)
+        owner = lax.rem(tm - d + tm_n, tm_n)
+        for k, part in ((i, wide_part(owner, 1 - core)), (i + 1, narrow_part(owner, 1 - core))):
+            remote(part, part, conv_fwd_send.at[k], conv_fwd_recv.at[k], sibling).wait_recv()
+
+    depth = narrow_ref.shape[0]
+    left = lax.broadcasted_iota(jnp.int32, (depth, 2 * thin), 1) < thin
+    for t in range(0, tm_n, 2):
+        a = narrow[t].astype(jnp.float32)
+        b = narrow[t + 1].astype(jnp.float32)
+        at = tm_n * wide + t * thin
+        kernel[0:depth, at : at + 2 * thin] = jnp.where(left, a, pltpu.roll(b, thin, 1)).astype(jnp.bfloat16)
+        kernel[depth:, at : at + 2 * thin] = jnp.where(left, pltpu.roll(a, thin, 1), b).astype(jnp.bfloat16)
+
+    for copy in weights:
+        copy.wait()
+
+    lane = lax.broadcasted_iota(jnp.int32, (line_rows, 128), 1)
+    mine = pl.ds(pl.multiple_of(core * line_rows, line_rows), line_rows)
+    other = pl.ds(pl.multiple_of((1 - core) * line_rows, line_rows), line_rows)
+    hid_at = pl.multiple_of(tp * hid_local, 128)
+
+    def h_part(s, owner):
+        return hidden.at[s, :, pl.ds(pl.multiple_of(owner * hid_local, 128), hid_local)]
+
+    def first_half(s, carry):
+        for d in range(1, line_n):
+            part = x_part(s, lax.rem(z - d + line_n, line_n))
+            remote(part, part, x_send.at[s, d - 1], x_recv.at[s, d - 1], sibling).wait_recv()
+        tail = xs[s, :, 4 * main :].astype(jnp.float32)
+        for q in range(4):
+            rows = slice(q * line_rows, (q + 1) * line_rows)
+            lhs[rows, :main] = xs[s, :, q * main : (q + 1) * main]
+            keep = (lane >= q * rem) & (lane < (q + 1) * rem)
+            lhs[rows, main:] = jnp.where(keep, tail, 0.0).astype(jnp.bfloat16)
+        for n in range(0, channels, 256):
+            embed[:, n : n + 256] = jnp.dot(lhs[...], kernel[:, n : n + 256], preferred_element_type=jnp.float32)
+        for q in range(4):
+            value = embed[q * line_rows : (q + 1) * line_rows, :]
+            mean = jnp.sum(value, axis=1, keepdims=True) * (1.0 / channels)
+            centred = value - mean
+            variance = jnp.sum(centred * centred, axis=1, keepdims=True) * (1.0 / channels)
+            normed = centred * lax.rsqrt(variance + EPS) * gain_ref[...] + shift_ref[...]
+            merged[s, mine, q * channels : (q + 1) * channels] = normed.astype(jnp.bfloat16)
+        to_sibling = remote(merged.at[s, mine], merged.at[s, mine], m_send.at[s], m_recv.at[s], sibling)
+        to_sibling.start()
+        remote(merged.at[s, other], merged.at[s, other], m_send.at[s], m_recv.at[s], sibling).wait_recv()
+        pre = jnp.dot(merged[s], win[...], preferred_element_type=jnp.float32) + bias_in_ref[...]
+        act = 0.5 * pre * (1.0 + lax.erf(pre * (0.5**0.5)))
+        hidden[s, :, pl.ds(hid_at, hid_local)] = act.astype(jnp.bfloat16)
+        for d in range(1, line_n):
+            remote(h_part(s, tp), h_part(s, tp), h_send.at[s, d - 1], h_recv.at[s, d - 1], along_line(d)).start()
+        remote(h_part(s, tp), h_part(s, tp), h_own_send.at[s], h_own_recv.at[s], sibling).start()
+        return carry
+
+    lax.fori_loop(0, blocks, first_half, 0)
+    weights_out.wait()
+
+    def line_owner(d, which):
+        return lax.rem(z - d + line_n, line_n) * 2 + which
+
+    def hand_over(s):
+        for d in range(1, line_n):
+            part = h_part(s, line_owner(d, core))
+            remote(part, part, h_send.at[s, d - 1], h_recv.at[s, d - 1], sibling).wait_recv()
+            remote(part, part, h_fwd_send.at[s, d - 1], h_fwd_recv.at[s, d - 1], sibling).start()
+
+    def second_half(s):
+        part = h_part(s, z * 2 + 1 - core)
+        remote(part, part, h_own_send.at[s], h_own_recv.at[s], sibling).wait_recv()
+        for d in range(1, line_n):
+            part = h_part(s, line_owner(d, 1 - core))
+            remote(part, part, h_fwd_send.at[s, d - 1], h_fwd_recv.at[s, d - 1], sibling).wait_recv()
+        pair, band = s // bands, lax.rem(s, bands)
+        for n in range(0, out_ref.shape[1], 256):
+            total = jnp.dot(hidden[s], wout[:, n : n + 256], preferred_element_type=jnp.float32)
+            result = (total + bias_out_ref[:, n : n + 256]).astype(jnp.bfloat16)
+            for c in range(2):
+                for l in range(line_n):
+                    at = ((pair * tp_n + l * 2 + c) * bands + band) * cols
+                    r = (c * line_n + l) * cols
+                    out_ref[pl.ds(pl.multiple_of(at, cols), cols), n : n + 256] = result[r : r + cols]
+
+    hand_over(0)
+
+    def finish(s, carry):
+        hand_over(s)
+        second_half(s - 1)
+        return carry
+
+    lax.fori_loop(1, blocks, finish, 0)
+    second_half(blocks - 1)
+
+    for copy in conv + forwards + pixels:
+        copy.wait_send()
+
+    def drain(s, carry):
+        remote(merged.at[s, mine], merged.at[s, mine], m_send.at[s], m_recv.at[s], sibling).wait_send()
+        remote(h_part(s, tp), h_part(s, tp), h_own_send.at[s], h_own_recv.at[s], sibling).wait_send()
+        for d in range(1, line_n):
+            part = h_part(s, tp)
+            remote(part, part, h_send.at[s, d - 1], h_recv.at[s, d - 1], along_line(d)).wait_send()
+            part = h_part(s, line_owner(d, core))
+            remote(part, part, h_fwd_send.at[s, d - 1], h_fwd_recv.at[s, d - 1], sibling).wait_send()
+        return carry
+
+    lax.fori_loop(0, blocks, drain, 0)
+
+
+def split_channels(vector, shards, wide):
+    parts = vector.reshape(shards, -1)
+    return jnp.concatenate([parts[:, :wide].reshape(-1), parts[:, wide:].reshape(-1)]).reshape(1, -1)
+
+
+def per_device_fused(pixels, conv_weight, norm_gain, norm_bias, proj_in, bias_in, proj_out, bias_out):
+    tm_n, tp_n = lax.axis_size("tm"), lax.axis_size("tp")
+    pairs, rows, grid_cols, patch = pixels.shape
+    channels = conv_weight.shape[1] * tm_n
+    bands, cols = rows // 2, grid_cols // 2
+    main = patch // 128 * 128
+    rem = patch - main
+    wide = conv_weight.shape[1] // 256 * 256
+    depth = main + 128
+
+    x = pixels.reshape(pairs, bands, 2, cols, 2, patch).transpose(0, 1, 3, 2, 4, 5).reshape(-1, 4, patch)
+    n_rows = x.shape[0]
+    x = jnp.concatenate(
+        [
+            x[:, :, :main].reshape(n_rows, 4 * main),
+            x[:, :, main:].reshape(n_rows, 4 * rem),
+            jnp.zeros((n_rows, 128 - 4 * rem), x.dtype),
+        ],
+        axis=1,
+    )
+    w_rem = conv_weight[main:]
+    w = jnp.concatenate(
+        [conv_weight[:main]] + [w_rem] * 4 + [jnp.zeros((128 - 4 * rem, w_rem.shape[1]), w_rem.dtype)], axis=0
+    )
+    w_wide = w[:, :wide]
+    w_narrow = jnp.concatenate([w[: depth // 2, wide:], w[depth // 2 :, wide:]], axis=1)
+
+    blocks = pairs * bands
+    line_n = tp_n // 2
+    group = tp_n * cols
+    bf16 = jnp.bfloat16
+    dma = pltpu.SemaphoreType.DMA
+    vmem = pl.BlockSpec(memory_space=pltpu.VMEM)
+    anywhere = pl.BlockSpec(memory_space=pl.ANY)
+    conv_sems = [dma((2 * (tm_n - 1),))] * 4
+    line_sems = dma((blocks, line_n - 1))
+    out = pl.pallas_call(
+        functools.partial(fused_kernel, (tm_n, tp_n, pairs, bands, cols, main, rem, channels)),
+        out_shape=jax.ShapeDtypeStruct((blocks * group, proj_out.shape[1]), bf16),
+        in_specs=[vmem] * 7 + [anywhere] * 2,
+        out_specs=vmem,
+        scratch_shapes=[
+            pltpu.VMEM((blocks, line_n * cols, x.shape[1]), bf16),
+            pltpu.VMEM((depth, channels), bf16),
+            pltpu.VMEM((tm_n,) + w_narrow.shape, bf16),
+            pltpu.VMEM((4 * line_n * cols, depth), bf16),
+            pltpu.VMEM((4 * line_n * cols, channels), jnp.float32),
+            pltpu.VMEM((blocks, group, 4 * channels), bf16),
+            pltpu.VMEM((blocks, group, proj_out.shape[0]), bf16),
+            pltpu.VMEM(proj_in.shape, bf16),
+            pltpu.VMEM(proj_out.shape, bf16),
+            dma((2 + blocks,)),
+            dma((8 * tm_n,)),
+            dma((1,)),
+        ]
+        + conv_sems
+        + [line_sems] * 2
+        + [dma((blocks,))] * 2
+        + [line_sems] * 2
+        + [dma((blocks,))] * 2
+        + [line_sems] * 2,
+        compiler_params=pltpu.CompilerParams(
+            collective_id=0, has_side_effects=True, vmem_limit_bytes=VMEM_BYTES
+        ),
+    )(
+        x, w_wide, w_narrow,
+        split_channels(norm_gain, tm_n, wide), split_channels(norm_bias, tm_n, wide),
+        bias_in.reshape(1, -1), bias_out.reshape(1, -1), proj_in, proj_out,
+    )
+    return out.reshape(pairs, tp_n * bands, cols, proj_out.shape[1])
+
+
+def fused_fits(pixels, conv_weight, proj_in, proj_out):
+    pairs, rows, grid_cols, patch = pixels.shape
+    tm_n, tp_n = lax.axis_size("tm"), lax.axis_size("tp")
+    local = conv_weight.shape[1]
+    held = 2 * (proj_in.size + proj_out.size) + 8 * pairs * tp_n * rows * grid_cols * local * tm_n // 2
+    return (
+        rows % 2 == 0
+        and grid_cols % 32 == 0
+        and tm_n % 2 == 0
+        and tp_n % 2 == 0
+        and tp_n >= 4
+        and local % 256 == 64
+        and patch % 128 != 0
+        and 4 * (patch % 128) <= 128
+        and proj_in.shape[1] % 128 == 0
+        and proj_out.shape[1] % 256 == 0
+        and held < VMEM_BYTES // 3 * 2
+    )
+
+
+def per_device(pixels, conv_weight, norm_gain, norm_bias, proj_in, bias_in, proj_out, bias_out):
+    if fused_fits(pixels, conv_weight, proj_in, proj_out):
+        body = per_device_fused
+    elif pixels.shape[1] % 2 == 0:
+        body = per_device_whole_blocks
+    else:
+        body = per_device_split_blocks
+    return body(pixels, conv_weight, norm_gain, norm_bias, proj_in, bias_in, proj_out, bias_out)
 
 
 def solution(mesh):

time: 204 us -> 131 us (0.64)
  waiting for transfers between devices: 161 us -> 0 us
  Pallas kernels: 0 us -> 119 us
  matrix products: 25 us -> 0 us
  between operations: 13.2 us -> 0.13 us
  local copies, waits for them, and re-layouts: 3.5 us -> 10.4 us
    all_gather x3 -> x0, waiting for transfers between devices: 161 us -> none  [the longest x1 56.1 us: per_device_whole_blocks(): lax.all_gather(merged, 'tp', axis=0, tiled=True)]
    pallas_call x0 -> x1, Pallas kernels: none -> 119 us  [per_device_fused(): pl.pallas_call(functools.partial(fused_kernel, (tm_n, tp_n, pairs, bands,...]
    dot_general x3 -> x0, matrix products: 25 us -> none  [the longest x1 12.1 us: per_device_whole_blocks(): jnp.dot(lax.all_gather(merged, 'tp', axis=0, tiled=True), proj_in, prefer...]
    unnamed x10 -> x18, local copies, waits for them, and re-layouts: 0.42 us -> 6.05 us
  transfers between devices with their start and end apart: 3 -> 0, of which waited for: 3 -> 0; matrix products, arithmetic and copies ran while one was open for 0% -> 0% of each run, Pallas kernels for 0% -> 0%
where the time goes in v2:
time: 131 us
  Pallas kernels  119 us (91%)
  local copies, waits for them, and re-layouts  10.4 us (8%)
    pallas_call x1, Pallas kernels, per_device_fused(): pl.pallas_call(functools.partial(fused_kernel, (tm_n, tp_n, pairs, bands,...  119 us
    unnamed x18, local copies, waits for them, and re-layouts  6.05 us

profile of v2, /device:TPU:0, one launch (start us, length us, event | category | flops | bytes accessed | tf_op | source)
XLA Modules:
  0.0 130.8 jit_solution(13160905232334558852)
XLA Ops:
  0.0 0.0 copy-start
  0.0 0.0 copy-start.1
  0.0 0.0 copy-start.2
  0.0 1.8 %copy.31 = bf16[1176,320]{1,0:T(8,128)(2,1)S(1)} copy(bf16[1176,320]{0,1:T(8,128)(2,1)} %param.9) | data formatting | bytes 1505280 | tf_op args[1]
  1.8 0.1 constant_dynamic-update-slice_fusion
  2.0 0.8 pad_maximum_fusion.narrow_ref
  2.8 0.9 slice.46.wide_ref
  3.7 1.8 %copy.25 = bf16[2,4,32,1176]{3,0,2,1:T(2,128)(2,1)S(1)} copy(bf16[2,4,32,1176]{3,2,1,0:T(8,128)(2,1)} %param.8) | data formatting | bytes 1204224 | tf_op args[0]
  5.4 0.1 copy.26
  5.6 0.1 copy.28
  5.7 0.1 copy.29
  5.8 1.0 concatenate.16.x_ref
  6.8 0.0 copy-done
  6.8 0.1 reshape.49
  6.9 0.1 reshape.51
  7.0 0.6 reshape.52.gain_ref
  7.6 0.0 copy-done.1
  7.6 0.1 reshape.53
  7.7 0.1 reshape.55
  7.8 0.6 reshape.56.shift_ref
  8.4 0.0 copy-done.2
  8.4 0.6 reshape.57.bias_in_ref
  9.0 119.5 %shard_map.82 = bf16[512,1024]{1,0:T(8,128)(2,1)} custom-call(bf16[64,4736]{1,0:T(8,128)(2,1)} %concatenate.16.x_ref, bf16[1280,256]{1,0:T(8,128)(2,1)} %slice.46.wide_ref, bf16[640,128]{1,0:T(8,128)(2,1)} %pad_maximum_fusion.narrow_ref, f32[1,1280]{1,0:T(1,128)} %reshape.52.gain_ref, f32[1,1280]{1,0:T(1,128)} %reshape.56.shift_ref, ...), custom_call_target="tpu_custom_call" | custom-call | tf_op jit(solution)/shard_map/pallas_call | solution.py:372
  128.5 2.3 %copy.41 = bf16[2,16,16,1024]{3,2,1,0:T(8,128)(2,1)} copy(bf16[2,16,16,1024]{3,2,1,0:T(8,128)(2,1)} %bitcast.16) | data formatting | bytes 2097152
  (18 shorter events, 0.2 us)
Async XLA Ops:
  0.0 6.8 %copy-start = (f32[1280]{0:T(1024)S(1)}, f32[1280]{0:T(1024)}, u32[]{:S(2)}) copy-start(f32[1280]{0:T(1024)} %param.10) | copy-start | bytes 15364
  0.0 7.6 %copy-start.1 = (f32[1280]{0:T(1024)S(1)}, f32[1280]{0:T(1024)}, u32[]{:S(2)}) copy-start(f32[1280]{0:T(1024)} %param.11) | copy-start | bytes 15364
  0.0 8.4 %copy-start.2 = (f32[640]{0:T(1024)S(1)}, f32[640]{0:T(1024)}, u32[]{:S(2)}) copy-start(f32[640]{0:T(1024)} %param.13) | copy-start | bytes 7684

commit v3 on v2

--- a/solution.py
+++ b/solution.py
@@ -116,8 +116,22 @@
     z = tp // 2
     sibling = (tm, z * 2 + 1 - core)
 
-    def along_line(d):
-        return (tm, lax.rem(z + d, line_n) * 2 + core)
+    def on_line(place):
+        return (tm, place * 2 + core)
+
+    last = line_n - 1
+    inner = (z > 0) & (z < last)
+    far_source = (2 - z) * last
+    far_target = (z - 1) * last
+
+    def each_reach(act):
+        for e in (2, -2, 1, -1):
+            place = z + e
+            pl.when((place >= 0) & (place <= last))(functools.partial(act, place))
+
+    def each_source(act):
+        for place in range(line_n):
+            pl.when(z != place)(functools.partial(act, place))
 
     def along_tm(d):
         return (lax.rem(tm + d, tm_n), tp)
@@ -129,7 +143,7 @@
 
     barrier = pltpu.get_barrier_semaphore()
     peers = [sibling]
-    peers += [along_line(d) for d in range(1, line_n)]
+    peers += [on_line(lax.rem(z + d, line_n)) for d in range(1, line_n)]
     peers += [along_tm(d) for d in range(1, tm_n)]
     for peer in peers:
         pl.semaphore_signal(barrier, inc=1, device_id=peer, device_id_type=MESH)
@@ -189,23 +203,34 @@
                 narrow_part(tm, core), conv_send.at[i + 1], conv_recv.at[i + 1], along_tm(d),
             )
         )
-    for copy in conv:
-        copy.start()
-
     def x_part(s, place):
         return xs.at[s, pl.ds(pl.multiple_of(place * cols, cols), cols)]
 
-    pixels = []
+    def x_copy(s, place):
+        return remote(
+            x_ref.at[pl.ds(s * cols, cols)], x_part(s, z), x_send.at[s, place], x_recv.at[s, z], on_line(place)
+        )
+
+    def x_arrival(s, place):
+        return remote(x_part(s, place), x_part(s, place), x_send.at[s, place], x_recv.at[s, place], sibling)
+
+    def x_pass_on(s):
+        part = x_part(s, far_source)
+        return remote(part, part, x_send.at[s, z], x_recv.at[s, far_source], on_line(far_target))
+
+    def pass_on_pixels(s):
+        @pl.when(inner)
+        def _():
+            x_arrival(s, far_source).wait_recv()
+            x_pass_on(s).start()
+
     for s in range(blocks):
-        for d in range(1, line_n):
-            pixels.append(
-                remote(
-                    x_ref.at[pl.ds(s * cols, cols)], x_part(s, z),
-                    x_send.at[s, d - 1], x_recv.at[s, d - 1], along_line(d),
-                )
-            )
-    for copy in pixels:
+        each_reach(lambda place, s=s: x_copy(s, place).start())
+        for copy in conv[2 * s : 2 * s + 2]:
+            copy.start()
+    for copy in conv[2 * blocks :]:
         copy.start()
+    pass_on_pixels(0)
 
     forwards = []
     for d in range(1, tm_n):
@@ -235,6 +260,7 @@
 
     for copy in weights:
         copy.wait()
+    pass_on_pixels(1)
 
     lane = lax.broadcasted_iota(jnp.int32, (line_rows, 128), 1)
     mine = pl.ds(pl.multiple_of(core * line_rows, line_rows), line_rows)
@@ -244,10 +270,26 @@
     def h_part(s, owner):
         return hidden.at[s, :, pl.ds(pl.multiple_of(owner * hid_local, 128), hid_local)]
 
+    def h_copy(s, place):
+        return remote(h_part(s, tp), h_part(s, tp), h_send.at[s, place], h_recv.at[s, z], on_line(place))
+
+    def h_arrival(s, place):
+        part = h_part(s, place * 2 + core)
+        return remote(part, part, h_send.at[s, place], h_recv.at[s, place], sibling)
+
+    def h_pass_on(s):
+        part = h_part(s, far_source * 2 + core)
+        return remote(part, part, h_send.at[s, z], h_recv.at[s, far_source], on_line(far_target))
+
+    def h_across(s, place, which):
+        part = h_part(s, place * 2 + which)
+        return remote(part, part, h_fwd_send.at[s, place], h_fwd_recv.at[s, place], sibling)
+
     def first_half(s, carry):
-        for d in range(1, line_n):
-            part = x_part(s, lax.rem(z - d + line_n, line_n))
-            remote(part, part, x_send.at[s, d - 1], x_recv.at[s, d - 1], sibling).wait_recv()
+        def arrived(place):
+            pl.when(jnp.logical_not(inner & (far_source == place)))(lambda: x_arrival(s, place).wait_recv())
+
+        each_source(arrived)
         tail = xs[s, :, 4 * main :].astype(jnp.float32)
         for q in range(4):
             rows = slice(q * line_rows, (q + 1) * line_rows)
@@ -269,29 +311,33 @@
         pre = jnp.dot(merged[s], win[...], preferred_element_type=jnp.float32) + bias_in_ref[...]
         act = 0.5 * pre * (1.0 + lax.erf(pre * (0.5**0.5)))
         hidden[s, :, pl.ds(hid_at, hid_local)] = act.astype(jnp.bfloat16)
-        for d in range(1, line_n):
-            remote(h_part(s, tp), h_part(s, tp), h_send.at[s, d - 1], h_recv.at[s, d - 1], along_line(d)).start()
+        each_reach(lambda place: h_copy(s, place).start())
         remote(h_part(s, tp), h_part(s, tp), h_own_send.at[s], h_own_recv.at[s], sibling).start()
+        pl.when(s + 2 < blocks)(lambda: pass_on_pixels(s + 2))
         return carry
 
     lax.fori_loop(0, blocks, first_half, 0)
     weights_out.wait()
 
-    def line_owner(d, which):
-        return lax.rem(z - d + line_n, line_n) * 2 + which
-
     def hand_over(s):
-        for d in range(1, line_n):
-            part = h_part(s, line_owner(d, core))
-            remote(part, part, h_send.at[s, d - 1], h_recv.at[s, d - 1], sibling).wait_recv()
-            remote(part, part, h_fwd_send.at[s, d - 1], h_fwd_recv.at[s, d - 1], sibling).start()
+        @pl.when(inner)
+        def _():
+            h_arrival(s, far_source).wait_recv()
+            h_pass_on(s).start()
+            h_across(s, far_source, core).start()
+
+        def arrived(place):
+            @pl.when(jnp.logical_not(inner & (far_source == place)))
+            def _():
+                h_arrival(s, place).wait_recv()
+                h_across(s, place, core).start()
+
+        each_source(arrived)
 
     def second_half(s):
         part = h_part(s, z * 2 + 1 - core)
         remote(part, part, h_own_send.at[s], h_own_recv.at[s], sibling).wait_recv()
-        for d in range(1, line_n):
-            part = h_part(s, line_owner(d, 1 - core))
-            remote(part, part, h_fwd_send.at[s, d - 1], h_fwd_recv.at[s, d - 1], sibling).wait_recv()
+        each_source(lambda place: h_across(s, place, 1 - core).wait_recv())
         pair, band = s // bands, lax.rem(s, bands)
         for n in range(0, out_ref.shape[1], 256):
             total = jnp.dot(hidden[s], wout[:, n : n + 256], preferred_element_type=jnp.float32)
@@ -312,17 +358,21 @@
     lax.fori_loop(1, blocks, finish, 0)
     second_half(blocks - 1)
 
-    for copy in conv + forwards + pixels:
+    for copy in conv + forwards:
         copy.wait_send()
 
     def drain(s, carry):
         remote(merged.at[s, mine], merged.at[s, mine], m_send.at[s], m_recv.at[s], sibling).wait_send()
         remote(h_part(s, tp), h_part(s, tp), h_own_send.at[s], h_own_recv.at[s], sibling).wait_send()
-        for d in range(1, line_n):
-            part = h_part(s, tp)
-            remote(part, part, h_send.at[s, d - 1], h_recv.at[s, d - 1], along_line(d)).wait_send()
-            part = h_part(s, line_owner(d, core))
-            remote(part, part, h_fwd_send.at[s, d - 1], h_fwd_recv.at[s, d - 1], sibling).wait_send()
+        each_reach(lambda place: x_copy(s, place).wait_send())
+        each_reach(lambda place: h_copy(s, place).wait_send())
+        each_source(lambda place: h_across(s, place, core).wait_send())
+
+        @pl.when(inner)
+        def _():
+            x_pass_on(s).wait_send()
+            h_pass_on(s).wait_send()
+
         return carry
 
     lax.fori_loop(0, blocks, drain, 0)
@@ -368,7 +418,7 @@
     vmem = pl.BlockSpec(memory_space=pltpu.VMEM)
     anywhere = pl.BlockSpec(memory_space=pl.ANY)
     conv_sems = [dma((2 * (tm_n - 1),))] * 4
-    line_sems = dma((blocks, line_n - 1))
+    line_sems = dma((blocks, line_n))
     out = pl.pallas_call(
         functools.partial(fused_kernel, (tm_n, tp_n, pairs, bands, cols, main, rem, channels)),
         out_shape=jax.ShapeDtypeStruct((blocks * group, proj_out.shape[1]), bf16),
@@ -415,7 +465,8 @@
         and grid_cols % 32 == 0
         and tm_n % 2 == 0
         and tp_n % 2 == 0
-        and tp_n >= 4
+        and tp_n == 8
+        and pairs * rows >= 4
         and local % 256 == 64
         and patch % 128 != 0
         and 4 * (patch % 128) <= 128

time: 131 us -> 109 us (0.83)
  Pallas kernels: 119 us -> 97.5 us
    pallas_call x1, Pallas kernels: 119 us -> 97.5 us  [per_device_fused(): pl.pallas_call(functools.partial(fused_kernel, (tm_n, tp_n, pairs, bands,...]
where the time goes in v3:
time: 109 us
  Pallas kernels  97.5 us (89%)
  local copies, waits for them, and re-layouts  10.4 us (10%)
    pallas_call x1, Pallas kernels, per_device_fused(): pl.pallas_call(functools.partial(fused_kernel, (tm_n, tp_n, pairs, bands,...  97.5 us
    unnamed x18, local copies, waits for them, and re-layouts  6.05 us

profile of v3, /device:TPU:0, one launch (start us, length us, event | category | flops | bytes accessed | tf_op | source)
XLA Modules:
  0.0 108.8 jit_solution(17074450251380806428)
XLA Ops:
  0.0 0.0 copy-start
  0.0 0.0 copy-start.1
  0.0 0.0 copy-start.2
  0.0 1.8 %copy.31 = bf16[1176,320]{1,0:T(8,128)(2,1)S(1)} copy(bf16[1176,320]{0,1:T(8,128)(2,1)} %param.9) | data formatting | bytes 1505280 | tf_op args[1]
  1.8 0.1 constant_dynamic-update-slice_fusion
  2.0 0.8 pad_maximum_fusion.narrow_ref
  2.8 0.9 slice.46.wide_ref
  3.7 1.8 %copy.25 = bf16[2,4,32,1176]{3,0,2,1:T(2,128)(2,1)S(1)} copy(bf16[2,4,32,1176]{3,2,1,0:T(8,128)(2,1)} %param.8) | data formatting | bytes 1204224 | tf_op args[0]
  5.4 0.1 copy.26
  5.6 0.1 copy.28
  5.7 0.1 copy.29
  5.8 1.0 concatenate.16.x_ref
  6.8 0.0 copy-done
  6.8 0.1 reshape.49
  6.9 0.1 reshape.51
  7.0 0.6 reshape.52.gain_ref
  7.6 0.0 copy-done.1
  7.6 0.1 reshape.53
  7.7 0.1 reshape.55
  7.8 0.6 reshape.56.shift_ref
  8.4 0.0 copy-done.2
  8.4 0.6 reshape.57.bias_in_ref
  9.0 97.5 %shard_map.82 = bf16[512,1024]{1,0:T(8,128)(2,1)} custom-call(bf16[64,4736]{1,0:T(8,128)(2,1)} %concatenate.16.x_ref, bf16[1280,256]{1,0:T(8,128)(2,1)} %slice.46.wide_ref, bf16[640,128]{1,0:T(8,128)(2,1)} %pad_maximum_fusion.narrow_ref, f32[1,1280]{1,0:T(1,128)} %reshape.52.gain_ref, f32[1,1280]{1,0:T(1,128)} %reshape.56.shift_ref, ...), custom_call_target="tpu_custom_call" | custom-call | tf_op jit(solution)/shard_map/pallas_call | solution.py:422
  106.5 2.3 %copy.41 = bf16[2,16,16,1024]{3,2,1,0:T(8,128)(2,1)} copy(bf16[2,16,16,1024]{3,2,1,0:T(8,128)(2,1)} %bitcast.16) | data formatting | bytes 2097152
  (18 shorter events, 0.2 us)
Async XLA Ops:
  0.0 6.8 %copy-start = (f32[1280]{0:T(1024)S(1)}, f32[1280]{0:T(1024)}, u32[]{:S(2)}) copy-start(f32[1280]{0:T(1024)} %param.10) | copy-start | bytes 15364
  0.0 7.6 %copy-start.1 = (f32[1280]{0:T(1024)S(1)}, f32[1280]{0:T(1024)}, u32[]{:S(2)}) copy-start(f32[1280]{0:T(1024)} %param.11) | copy-start | bytes 15364
  0.0 8.4 %copy-start.2 = (f32[640]{0:T(1024)S(1)}, f32[640]{0:T(1024)}, u32[]{:S(2)}) copy-start(f32[640]{0:T(1024)} %param.13) | copy-start | bytes 7684

commit v4 on v3

--- a/solution.py
+++ b/solution.py
@@ -93,10 +93,10 @@
 
 def fused_kernel(
     dims,
-    x_ref, wide_ref, narrow_ref, gain_ref, shift_ref, bias_in_ref, bias_out_ref, proj_in_ref, proj_out_ref,
+    raw_ref, shard_ref, gain_ref, shift_ref, bias_in_ref, bias_out_ref, proj_in_ref, proj_out_ref,
     out_ref,
-    xs, kernel, narrow, lhs, embed, merged, hidden, win, wout,
-    own_sems, win_sems, wout_sem,
+    x_ref, xs, turned, kernel, lhs, embed, merged, hidden, win, wout,
+    own_sems, weight_sems,
     conv_send, conv_recv, conv_fwd_send, conv_fwd_recv,
     x_send, x_recv, m_send, m_recv,
     h_send, h_recv, h_own_send, h_own_recv, h_fwd_send, h_fwd_recv,
@@ -106,10 +106,8 @@
     blocks = pairs * bands
     line_rows = line_n * cols
     hid_local = proj_in_ref.shape[1]
-    wide = wide_ref.shape[1]
-    thin = channels // tm_n - wide
-    half_wide = wide_ref.shape[0] // 2
-    half_narrow = narrow_ref.shape[0] // 2
+    share = shard_ref.shape[0]
+    half = share // 2
     tm = lax.axis_index("tm")
     tp = lax.axis_index("tp")
     core = lax.rem(tp, 2)
@@ -148,67 +146,52 @@
     for peer in peers:
         pl.semaphore_signal(barrier, inc=1, device_id=peer, device_id_type=MESH)
 
-    own = [
-        pltpu.make_async_copy(wide_ref, kernel.at[:, pl.ds(pl.multiple_of(tm * wide, wide), wide)], own_sems.at[0]),
-        pltpu.make_async_copy(narrow_ref, narrow.at[tm], own_sems.at[1]),
+    weights = pltpu.make_async_copy(proj_in_ref, win, weight_sems.at[0])
+    weights_out = pltpu.make_async_copy(proj_out_ref, wout, weight_sems.at[1])
+    own_shard = pltpu.make_async_copy(
+        shard_ref, turned.at[pl.ds(pl.multiple_of(tm * share, 16), share)], own_sems.at[0]
+    )
+    for copy in (own_shard, weights, weights_out):
+        copy.start()
+
+    lane = lax.broadcasted_iota(jnp.int32, (cols, 128), 1)
+    for s in range(blocks):
+        tail = jnp.zeros((cols, 128), jnp.float32)
+        for g in range(4):
+            rows = slice(g * cols, (g + 1) * cols)
+            x_ref[s, :, g * main : (g + 1) * main] = raw_ref[s, rows, :main]
+            end = raw_ref[s, rows, main:].astype(jnp.float32)
+            end = jnp.concatenate([end, jnp.zeros((cols, 128 - rem), jnp.float32)], axis=1)
+            tail += pltpu.roll(end, g * rem, 1) if g else end
+        x_ref[s, :, 4 * main :] = tail.astype(jnp.bfloat16)
+    own_blocks = [
+        pltpu.make_async_copy(
+            x_ref.at[s], xs.at[s, pl.ds(pl.multiple_of(z * cols, cols), cols)], own_sems.at[1 + s]
+        )
+        for s in range(blocks)
     ]
-    for s in range(blocks):
-        own.append(
-            pltpu.make_async_copy(
-                x_ref.at[pl.ds(s * cols, cols)],
-                xs.at[s, pl.ds(pl.multiple_of(z * cols, cols), cols)],
-                own_sems.at[2 + s],
-            )
-        )
-    weights = []
-    for q in range(4):
-        for t in range(tm_n):
-            first = q * channels + t * (wide + thin)
-            for src, dst, count in (
-                (first, q * channels + t * wide, wide),
-                (first + wide, q * channels + tm_n * wide + t * thin, thin),
-            ):
-                weights.append(
-                    pltpu.make_async_copy(
-                        proj_in_ref.at[pl.ds(src, count)], win.at[pl.ds(dst, count)], win_sems.at[len(weights)]
-                    )
-                )
-    weights_out = pltpu.make_async_copy(proj_out_ref, wout, wout_sem.at[0])
-    for copy in own + weights + [weights_out]:
+    for copy in own_blocks:
         copy.start()
 
     pl.semaphore_wait(barrier, len(peers))
 
-    def wide_part(owner, half):
-        return kernel.at[
-            pl.ds(pl.multiple_of(half * half_wide, 16), half_wide),
-            pl.ds(pl.multiple_of(owner * wide, wide), wide),
-        ]
-
-    def narrow_part(owner, half):
-        return narrow.at[owner, pl.ds(pl.multiple_of(half * half_narrow, 16), half_narrow)]
-
-    conv = []
-    for d in range(1, tm_n):
-        i = 2 * (d - 1)
-        conv.append(
-            remote(
-                wide_ref.at[pl.ds(pl.multiple_of(core * half_wide, 16), half_wide)],
-                wide_part(tm, core), conv_send.at[i], conv_recv.at[i], along_tm(d),
-            )
-        )
-        conv.append(
-            remote(
-                narrow_ref.at[pl.ds(pl.multiple_of(core * half_narrow, 16), half_narrow)],
-                narrow_part(tm, core), conv_send.at[i + 1], conv_recv.at[i + 1], along_tm(d),
-            )
-        )
+    def shard_part(owner, which):
+        return turned.at[pl.ds(pl.multiple_of(owner * share + which * half, 16), half)]
+
+    conv = [
+        remote(
+            shard_ref.at[pl.ds(pl.multiple_of(core * half, 16), half)],
+            shard_part(tm, core), conv_send.at[d - 1], conv_recv.at[d - 1], along_tm(d),
+        )
+        for d in range(1, tm_n)
+    ]
+
     def x_part(s, place):
         return xs.at[s, pl.ds(pl.multiple_of(place * cols, cols), cols)]
 
     def x_copy(s, place):
         return remote(
-            x_ref.at[pl.ds(s * cols, cols)], x_part(s, z), x_send.at[s, place], x_recv.at[s, z], on_line(place)
+            x_ref.at[s], x_part(s, z), x_send.at[s, place], x_recv.at[s, z], on_line(place)
         )
 
     def x_arrival(s, place):
@@ -226,43 +209,29 @@
 
     for s in range(blocks):
         each_reach(lambda place, s=s: x_copy(s, place).start())
-        for copy in conv[2 * s : 2 * s + 2]:
+        for copy in conv[s : s + 1]:
             copy.start()
-    for copy in conv[2 * blocks :]:
+    for copy in conv[blocks:]:
         copy.start()
     pass_on_pixels(0)
 
     forwards = []
     for d in range(1, tm_n):
-        i = 2 * (d - 1)
-        owner = lax.rem(tm - d + tm_n, tm_n)
-        for k, part in ((i, wide_part(owner, core)), (i + 1, narrow_part(owner, core))):
-            remote(part, part, conv_send.at[k], conv_recv.at[k], sibling).wait_recv()
-            copy = remote(part, part, conv_fwd_send.at[k], conv_fwd_recv.at[k], sibling)
-            copy.start()
-            forwards.append(copy)
-    for copy in own:
+        part = shard_part(lax.rem(tm - d + tm_n, tm_n), core)
+        remote(part, part, conv_send.at[d - 1], conv_recv.at[d - 1], sibling).wait_recv()
+        copy = remote(part, part, conv_fwd_send.at[d - 1], conv_fwd_recv.at[d - 1], sibling)
+        copy.start()
+        forwards.append(copy)
+    own_shard.wait()
+    for d in range(1, tm_n):
+        part = shard_part(lax.rem(tm - d + tm_n, tm_n), 1 - core)
+        remote(part, part, conv_fwd_send.at[d - 1], conv_fwd_recv.at[d - 1], sibling).wait_recv()
+    for copy in own_blocks:
         copy.wait()
-    for d in range(1, tm_n):
-        i = 2 * (d - 1)
-        owner = lax.rem(tm - d + tm_n, tm_n)
-        for k, part in ((i, wide_part(owner, 1 - core)), (i + 1, narrow_part(owner, 1 - core))):
-            remote(part, part, conv_fwd_send.at[k], conv_fwd_recv.at[k], sibling).wait_recv()
-
-    depth = narrow_ref.shape[0]
-    left = lax.broadcasted_iota(jnp.int32, (depth, 2 * thin), 1) < thin
-    for t in range(0, tm_n, 2):
-        a = narrow[t].astype(jnp.float32)
-        b = narrow[t + 1].astype(jnp.float32)
-        at = tm_n * wide + t * thin
-        kernel[0:depth, at : at + 2 * thin] = jnp.where(left, a, pltpu.roll(b, thin, 1)).astype(jnp.bfloat16)
-        kernel[depth:, at : at + 2 * thin] = jnp.where(left, pltpu.roll(a, thin, 1), b).astype(jnp.bfloat16)
-
-    for copy in weights:
-        copy.wait()
+    kernel[...] = turned[...].T
+    weights.wait()
     pass_on_pixels(1)
 
-    lane = lax.broadcasted_iota(jnp.int32, (line_rows, 128), 1)
     mine = pl.ds(pl.multiple_of(core * line_rows, line_rows), line_rows)
     other = pl.ds(pl.multiple_of((1 - core) * line_rows, line_rows), line_rows)
     hid_at = pl.multiple_of(tp * hid_local, 128)
@@ -291,20 +260,28 @@
 
         each_source(arrived)
         tail = xs[s, :, 4 * main :].astype(jnp.float32)
-        for q in range(4):
-            rows = slice(q * line_rows, (q + 1) * line_rows)
-            lhs[rows, :main] = xs[s, :, q * main : (q + 1) * main]
-            keep = (lane >= q * rem) & (lane < (q + 1) * rem)
-            lhs[rows, main:] = jnp.where(keep, tail, 0.0).astype(jnp.bfloat16)
+        for g in range(4):
+            rows = slice(g * line_rows, (g + 1) * line_rows)
+            lhs[rows, :main] = xs[s, :, g * main : (g + 1) * main]
+            end = pltpu.roll(tail, 128 - g * rem, 1) if g else tail
+            lhs[rows, main:] = end[:, :rem].astype(jnp.bfloat16)
         for n in range(0, channels, 256):
-            embed[:, n : n + 256] = jnp.dot(lhs[...], kernel[:, n : n + 256], preferred_element_type=jnp.float32)
-        for q in range(4):
-            value = embed[q * line_rows : (q + 1) * line_rows, :]
-            mean = jnp.sum(value, axis=1, keepdims=True) * (1.0 / channels)
-            centred = value - mean
-            variance = jnp.sum(centred * centred, axis=1, keepdims=True) * (1.0 / channels)
-            normed = centred * lax.rsqrt(variance + EPS) * gain_ref[...] + shift_ref[...]
-            merged[s, mine, q * channels : (q + 1) * channels] = normed.astype(jnp.bfloat16)
+            part = jnp.dot(lhs[...], kernel[:, n : n + 256], preferred_element_type=jnp.float32)
+            embed[n // 128] = part[:, :128]
+            embed[n // 128 + 1] = part[:, 128:]
+        part_rows = line_rows // 2
+        for i in range(2):
+            for j in range(2):
+                for h in range(2):
+                    every = pl.ds((2 * i + h) * line_rows + j, part_rows, stride=2)
+                    value = jnp.concatenate([embed[k, every, :] for k in range(channels // 128)], axis=1)
+                    mean = jnp.sum(value, axis=1, keepdims=True) * (1.0 / channels)
+                    centred = value - mean
+                    variance = jnp.sum(centred * centred, axis=1, keepdims=True) * (1.0 / channels)
+                    normed = centred * lax.rsqrt(variance + EPS) * gain_ref[...] + shift_ref[...]
+                    at = pl.ds(pl.multiple_of(core * line_rows + h * part_rows, part_rows), part_rows)
+                    q = 2 * i + j
+                    merged[s, at, q * channels : (q + 1) * channels] = normed.astype(jnp.bfloat16)
         to_sibling = remote(merged.at[s, mine], merged.at[s, mine], m_send.at[s], m_recv.at[s], sibling)
         to_sibling.start()
         remote(merged.at[s, other], merged.at[s, other], m_send.at[s], m_recv.at[s], sibling).wait_recv()
@@ -341,12 +318,15 @@
         pair, band = s // bands, lax.rem(s, bands)
         for n in range(0, out_ref.shape[1], 256):
             total = jnp.dot(hidden[s], wout[:, n : n + 256], preferred_element_type=jnp.float32)
-            result = (total + bias_out_ref[:, n : n + 256]).astype(jnp.bfloat16)
+            result = total + bias_out_ref[:, n : n + 256]
             for c in range(2):
                 for l in range(line_n):
                     at = ((pair * tp_n + l * 2 + c) * bands + band) * cols
-                    r = (c * line_n + l) * cols
-                    out_ref[pl.ds(pl.multiple_of(at, cols), cols), n : n + 256] = result[r : r + cols]
+                    low = c * line_rows + l * (cols // 2)
+                    high = low + line_rows // 2
+                    tokens = [result[low : low + cols // 2], result[high : high + cols // 2]]
+                    tokens = jnp.concatenate(tokens, axis=0).astype(jnp.bfloat16)
+                    out_ref[pl.ds(pl.multiple_of(at, cols), cols), n : n + 256] = tokens
 
     hand_over(0)
 
@@ -376,11 +356,6 @@
         return carry
 
     lax.fori_loop(0, blocks, drain, 0)
-
-
-def split_channels(vector, shards, wide):
-    parts = vector.reshape(shards, -1)
-    return jnp.concatenate([parts[:, :wide].reshape(-1), parts[:, wide:].reshape(-1)]).reshape(1, -1)
 
 
 def per_device_fused(pixels, conv_weight, norm_gain, norm_bias, proj_in, bias_in, proj_out, bias_out):
@@ -390,26 +365,6 @@
     bands, cols = rows // 2, grid_cols // 2
     main = patch // 128 * 128
     rem = patch - main
-    wide = conv_weight.shape[1] // 256 * 256
-    depth = main + 128
-
-    x = pixels.reshape(pairs, bands, 2, cols, 2, patch).transpose(0, 1, 3, 2, 4, 5).reshape(-1, 4, patch)
-    n_rows = x.shape[0]
-    x = jnp.concatenate(
-        [
-            x[:, :, :main].reshape(n_rows, 4 * main),
-            x[:, :, main:].reshape(n_rows, 4 * rem),
-            jnp.zeros((n_rows, 128 - 4 * rem), x.dtype),
-        ],
-        axis=1,
-    )
-    w_rem = conv_weight[main:]
-    w = jnp.concatenate(
-        [conv_weight[:main]] + [w_rem] * 4 + [jnp.zeros((128 - 4 * rem, w_rem.shape[1]), w_rem.dtype)], axis=0
-    )
-    w_wide = w[:, :wide]
-    w_narrow = jnp.concatenate([w[: depth // 2, wide:], w[depth // 2 :, wide:]], axis=1)
-
     blocks = pairs * bands
     line_n = tp_n // 2
     group = tp_n * cols
@@ -417,26 +372,27 @@
     dma = pltpu.SemaphoreType.DMA
     vmem = pl.BlockSpec(memory_space=pltpu.VMEM)
     anywhere = pl.BlockSpec(memory_space=pl.ANY)
-    conv_sems = [dma((2 * (tm_n - 1),))] * 4
+    conv_sems = [dma((tm_n - 1,))] * 4
+    packed = 4 * main + 128
     line_sems = dma((blocks, line_n))
     out = pl.pallas_call(
         functools.partial(fused_kernel, (tm_n, tp_n, pairs, bands, cols, main, rem, channels)),
         out_shape=jax.ShapeDtypeStruct((blocks * group, proj_out.shape[1]), bf16),
-        in_specs=[vmem] * 7 + [anywhere] * 2,
+        in_specs=[vmem] * 6 + [anywhere] * 2,
         out_specs=vmem,
         scratch_shapes=[
-            pltpu.VMEM((blocks, line_n * cols, x.shape[1]), bf16),
-            pltpu.VMEM((depth, channels), bf16),
-            pltpu.VMEM((tm_n,) + w_narrow.shape, bf16),
-            pltpu.VMEM((4 * line_n * cols, depth), bf16),
-            pltpu.VMEM((4 * line_n * cols, channels), jnp.float32),
+            pltpu.VMEM((blocks, cols, packed), bf16),
+            pltpu.VMEM((blocks, line_n * cols, packed), bf16),
+            pltpu.VMEM((channels, patch), bf16),
+            pltpu.VMEM((patch, channels), bf16),
+            pltpu.VMEM((4 * line_n * cols, patch), bf16),
+            pltpu.VMEM((channels // 128, 4 * line_n * cols, 128), jnp.float32),
             pltpu.VMEM((blocks, group, 4 * channels), bf16),
             pltpu.VMEM((blocks, group, proj_out.shape[0]), bf16),
             pltpu.VMEM(proj_in.shape, bf16),
             pltpu.VMEM(proj_out.shape, bf16),
-            dma((2 + blocks,)),
-            dma((8 * tm_n,)),
-            dma((1,)),
+            dma((1 + blocks,)),
+            dma((2,)),
         ]
         + conv_sems
         + [line_sems] * 2
@@ -448,8 +404,8 @@
             collective_id=0, has_side_effects=True, vmem_limit_bytes=VMEM_BYTES
         ),
     )(
-        x, w_wide, w_narrow,
-        split_channels(norm_gain, tm_n, wide), split_channels(norm_bias, tm_n, wide),
+        pixels.reshape(blocks, 2 * grid_cols, patch), conv_weight.T,
+        norm_gain.reshape(1, -1), norm_bias.reshape(1, -1),
         bias_in.reshape(1, -1), bias_out.reshape(1, -1), proj_in, proj_out,
     )
     return out.reshape(pairs, tp_n * bands, cols, proj_out.shape[1])
@@ -463,11 +419,12 @@
     return (
         rows % 2 == 0
         and grid_cols % 32 == 0
-        and tm_n % 2 == 0
+        and tm_n >= 2
         and tp_n % 2 == 0
         and tp_n == 8
         and pairs * rows >= 4
-        and local % 256 == 64
+        and local % 32 == 0
+        and local * tm_n % 256 == 0
         and patch % 128 != 0
         and 4 * (patch % 128) <= 128
         and proj_in.shape[1] % 128 == 0

time: 109 us -> 104 us (0.954)
  local copies, waits for them, and re-layouts: 10.4 us -> 6.16 us
    unnamed x18 -> x1, local copies, waits for them, and re-layouts: 6.05 us -> 2.31 us
    reshape x8 -> x2, local copies, waits for them, and re-layouts: 1.64 us -> 2.58 us  [the longest x1 1.29 us: per_device_fused(): norm_gain.reshape(1, -1)]
where the time goes in v4:
time: 104 us; the launch traced here: 103 us
  Pallas kernels  97.2 us (93%)
  local copies, waits for them, and re-layouts  6.16 us (6%)
    pallas_call x1, Pallas kernels, per_device_fused(): pl.pallas_call(functools.partial(fused_kernel, (tm_n, tp_n, pairs, bands,...  97.2 us
    unnamed x1, local copies, waits for them, and re-layouts  2.31 us

profile of v4, /device:TPU:0, one launch (start us, length us, event | category | flops | bytes accessed | tf_op | source)
XLA Modules:
  0.0 103.4 jit_solution(2053156951482265059)
XLA Ops:
  0.0 1.3 %reshape.21.bias_in_ref = f32[1,640]{1,0:T(1,128)} reshape(f32[640]{0:T(1024)} %param.13) | data formatting | bytes 5120 | tf_op jit(solution)/shard_map/reshape | solution.py:409
  1.3 1.3 %reshape.19.gain_ref = f32[1,1280]{1,0:T(1,128)} reshape(f32[1280]{0:T(1024)} %param.10) | data formatting | bytes 10240 | tf_op jit(solution)/shard_map/reshape | solution.py:408
  2.6 1.3 %reshape.20.shift_ref = f32[1,1280]{1,0:T(1,128)} reshape(f32[1280]{0:T(1024)} %param.11) | data formatting | bytes 10240 | tf_op jit(solution)/shard_map/reshape | solution.py:408
  3.9 97.2 %shard_map.82 = bf16[512,1024]{1,0:T(8,128)(2,1)} custom-call(bf16[4,64,1176]{2,1,0:T(8,128)(2,1)} %bitcast.6, bf16[320,1176]{1,0:T(8,128)(2,1)} %bitcast.5, f32[1,1280]{1,0:T(1,128)} %reshape.19.gain_ref, f32[1,1280]{1,0:T(1,128)} %reshape.20.shift_ref, f32[1,640]{1,0:T(1,128)} %reshape.21.bias_in_ref, f32[1,1024]{1,0:T(1,128)} %bitcast.7, ...), custom_call_target="tpu_custom_call" | custom-call | tf_op jit(solution)/shard_map/pallas_call | solution.py:378
  101.1 2.3 %copy.10 = bf16[2,16,16,1024]{3,2,1,0:T(8,128)(2,1)} copy(bf16[2,16,16,1024]{3,2,1,0:T(8,128)(2,1)} %bitcast.4) | data formatting | bytes 2097152

commit v5 on v4

--- a/solution.py
+++ b/solution.py
@@ -254,7 +254,16 @@
         part = h_part(s, place * 2 + which)
         return remote(part, part, h_fwd_send.at[s, place], h_fwd_recv.at[s, place], sibling)
 
-    def first_half(s, carry):
+    def pass_on_hidden(s):
+        @pl.when(inner)
+        def _():
+            h_arrival(s, far_source).wait_recv()
+            h_pass_on(s).start()
+
+    gain, shift = gain_ref[...].reshape(1, -1), shift_ref[...].reshape(1, -1)
+    bias_in, bias_out = bias_in_ref[...].reshape(1, -1), bias_out_ref[...].reshape(1, -1)
+
+    def embed_block(s):
         def arrived(place):
             pl.when(jnp.logical_not(inner & (far_source == place)))(lambda: x_arrival(s, place).wait_recv())
 
@@ -278,30 +287,34 @@
                     mean = jnp.sum(value, axis=1, keepdims=True) * (1.0 / channels)
                     centred = value - mean
                     variance = jnp.sum(centred * centred, axis=1, keepdims=True) * (1.0 / channels)
-                    normed = centred * lax.rsqrt(variance + EPS) * gain_ref[...] + shift_ref[...]
+                    normed = centred * lax.rsqrt(variance + EPS) * gain + shift
                     at = pl.ds(pl.multiple_of(core * line_rows + h * part_rows, part_rows), part_rows)
                     q = 2 * i + j
                     merged[s, at, q * channels : (q + 1) * channels] = normed.astype(jnp.bfloat16)
         to_sibling = remote(merged.at[s, mine], merged.at[s, mine], m_send.at[s], m_recv.at[s], sibling)
         to_sibling.start()
+
+    def hidden_block(s):
         remote(merged.at[s, other], merged.at[s, other], m_send.at[s], m_recv.at[s], sibling).wait_recv()
-        pre = jnp.dot(merged[s], win[...], preferred_element_type=jnp.float32) + bias_in_ref[...]
+        pre = jnp.dot(merged[s], win[...], preferred_element_type=jnp.float32) + bias_in
         act = 0.5 * pre * (1.0 + lax.erf(pre * (0.5**0.5)))
         hidden[s, :, pl.ds(hid_at, hid_local)] = act.astype(jnp.bfloat16)
         each_reach(lambda place: h_copy(s, place).start())
         remote(h_part(s, tp), h_part(s, tp), h_own_send.at[s], h_own_recv.at[s], sibling).start()
+
+    def first_half(s, carry):
+        pl.when(s < blocks)(lambda: embed_block(s))
         pl.when(s + 2 < blocks)(lambda: pass_on_pixels(s + 2))
+        pl.when(s > 0)(lambda: hidden_block(s - 1))
+        pl.when(s > 2)(lambda: pass_on_hidden(s - 3))
         return carry
 
-    lax.fori_loop(0, blocks, first_half, 0)
+    lax.fori_loop(0, blocks + 1, first_half, 0)
     weights_out.wait()
 
     def hand_over(s):
-        @pl.when(inner)
-        def _():
-            h_arrival(s, far_source).wait_recv()
-            h_pass_on(s).start()
-            h_across(s, far_source, core).start()
+        pl.when(s >= blocks - 2)(lambda: pass_on_hidden(s))
+        pl.when(inner)(lambda: h_across(s, far_source, core).start())
 
         def arrived(place):
             @pl.when(jnp.logical_not(inner & (far_source == place)))
@@ -318,7 +331,7 @@
         pair, band = s // bands, lax.rem(s, bands)
         for n in range(0, out_ref.shape[1], 256):
             total = jnp.dot(hidden[s], wout[:, n : n + 256], preferred_element_type=jnp.float32)
-            result = total + bias_out_ref[:, n : n + 256]
+            result = total + bias_out[:, n : n + 256]
             for c in range(2):
                 for l in range(line_n):
                     at = ((pair * tp_n + l * 2 + c) * bands + band) * cols
@@ -405,8 +418,7 @@
         ),
     )(
         pixels.reshape(blocks, 2 * grid_cols, patch), conv_weight.T,
-        norm_gain.reshape(1, -1), norm_bias.reshape(1, -1),
-        bias_in.reshape(1, -1), bias_out.reshape(1, -1), proj_in, proj_out,
+        norm_gain, norm_bias, bias_in, bias_out, proj_in, proj_out,
     )
     return out.reshape(pairs, tp_n * bands, cols, proj_out.shape[1])
 

time: 104 us -> 99.3 us (0.955)
  local copies, waits for them, and re-layouts: 6.16 us -> 2.31 us
    reshape x3 -> x0, local copies, waits for them, and re-layouts: 3.86 us -> none  [the longest x1 1.29 us: per_device_fused(): norm_gain.reshape(1, -1)]
where the time goes in v5:
time: 99.3 us; the launch traced here: 99.1 us
  Pallas kernels  96.8 us (97%)
  local copies, waits for them, and re-layouts  2.31 us (2%)
    pallas_call x1, Pallas kernels, per_device_fused(): pl.pallas_call(functools.partial(fused_kernel, (tm_n, tp_n, pairs, bands,...  96.8 us
    unnamed x1, local copies, waits for them, and re-layouts  2.31 us

profile of v5, /device:TPU:0, one launch (start us, length us, event | category | flops | bytes accessed | tf_op | source)
XLA Modules:
  0.0 99.1 jit_solution(16930724326362509848)
XLA Ops:
  0.0 96.8 %shard_map.82 = bf16[512,1024]{1,0:T(8,128)(2,1)} custom-call(bf16[4,64,1176]{2,1,0:T(8,128)(2,1)} %bitcast.5, bf16[320,1176]{1,0:T(8,128)(2,1)} %bitcast.4, f32[1280]{0:T(1024)} %gain_ref.1, f32[1280]{0:T(1024)} %shift_ref.1, f32[640]{0:T(1024)} %bias_in_ref.1, f32[1024]{0:T(1024)} %bias_out_ref.1, bf16[5120,640]{1,0:T(8,128)(2,1)} %proj_in_ref.1, ...), custom_call_target="tpu_custom_call" | custom-call | tf_op jit(solution)/shard_map/pallas_call | solution.py:391
  96.8 2.3 %copy.10 = bf16[2,16,16,1024]{3,2,1,0:T(8,128)(2,1)} copy(bf16[2,16,16,1024]{3,2,1,0:T(8,128)(2,1)} %bitcast.3) | data formatting | bytes 2097152

commit v6 on v5

--- a/solution.py
+++ b/solution.py
@@ -207,13 +207,18 @@
             x_arrival(s, far_source).wait_recv()
             x_pass_on(s).start()
 
-    for s in range(blocks):
-        each_reach(lambda place, s=s: x_copy(s, place).start())
-        for copy in conv[s : s + 1]:
-            copy.start()
-    for copy in conv[blocks:]:
+    def send_pixels(s):
+        if s >= 2:
+            each_reach(lambda place: x_copy(s - 2, place).wait_send())
+        if s < blocks:
+            each_reach(lambda place: x_copy(s, place).start())
+
+    send_pixels(0)
+    for copy in conv:
         copy.start()
+    send_pixels(1)
     pass_on_pixels(0)
+    send_pixels(2)
 
     forwards = []
     for d in range(1, tm_n):
@@ -228,9 +233,11 @@
         remote(part, part, conv_fwd_send.at[d - 1], conv_fwd_recv.at[d - 1], sibling).wait_recv()
     for copy in own_blocks:
         copy.wait()
+    pass_on_pixels(1)
+    for s in range(3, blocks):
+        send_pixels(s)
     kernel[...] = turned[...].T
     weights.wait()
-    pass_on_pixels(1)
 
     mine = pl.ds(pl.multiple_of(core * line_rows, line_rows), line_rows)
     other = pl.ds(pl.multiple_of((1 - core) * line_rows, line_rows), line_rows)
@@ -354,10 +361,12 @@
     for copy in conv + forwards:
         copy.wait_send()
 
+    for s in range(max(blocks, 3), blocks + 2):
+        send_pixels(s)
+
     def drain(s, carry):
         remote(merged.at[s, mine], merged.at[s, mine], m_send.at[s], m_recv.at[s], sibling).wait_send()
         remote(h_part(s, tp), h_part(s, tp), h_own_send.at[s], h_own_recv.at[s], sibling).wait_send()
-        each_reach(lambda place: x_copy(s, place).wait_send())
         each_reach(lambda place: h_copy(s, place).wait_send())
         each_source(lambda place: h_across(s, place, core).wait_send())
 

time: 99.3 us -> 99.6 us (level)
  no operation moved by 1% of the time
where the time goes in v6:
time: 99.6 us; the launch traced here: 99.4 us
  Pallas kernels  97.1 us (97%)
  local copies, waits for them, and re-layouts  2.31 us (2%)
    pallas_call x1, Pallas kernels, per_device_fused(): pl.pallas_call(functools.partial(fused_kernel, (tm_n, tp_n, pairs, bands,...  97.1 us
    unnamed x1, local copies, waits for them, and re-layouts  2.31 us

profile of v6, /device:TPU:0, one launch (start us, length us, event | category | flops | bytes accessed | tf_op | source)
XLA Modules:
  0.0 99.4 jit_solution(10971142074108501774)
XLA Ops:
  0.0 97.1 %shard_map.82 = bf16[512,1024]{1,0:T(8,128)(2,1)} custom-call(bf16[4,64,1176]{2,1,0:T(8,128)(2,1)} %bitcast.5, bf16[320,1176]{1,0:T(8,128)(2,1)} %bitcast.4, f32[1280]{0:T(1024)} %gain_ref.1, f32[1280]{0:T(1024)} %shift_ref.1, f32[640]{0:T(1024)} %bias_in_ref.1, f32[1024]{0:T(1024)} %bias_out_ref.1, bf16[5120,640]{1,0:T(8,128)(2,1)} %proj_in_ref.1, ...), custom_call_target="tpu_custom_call" | custom-call | tf_op jit(solution)/shard_map/pallas_call | solution.py:400
  97.1 2.3 %copy.10 = bf16[2,16,16,1024]{3,2,1,0:T(8,128)(2,1)} copy(bf16[2,16,16,1024]{3,2,1,0:T(8,128)(2,1)} %bitcast.3) | data formatting | bytes 2097152

commit v7 on v5

--- a/solution.py
+++ b/solution.py
@@ -95,7 +95,7 @@
     dims,
     raw_ref, shard_ref, gain_ref, shift_ref, bias_in_ref, bias_out_ref, proj_in_ref, proj_out_ref,
     out_ref,
-    x_ref, xs, turned, kernel, lhs, embed, merged, hidden, win, wout,
+    x_ref, xs, turned, kernel, lhs, embed, merged, hidden, win, wout, total,
     own_sems, weight_sems,
     conv_send, conv_recv, conv_fwd_send, conv_fwd_recv,
     x_send, x_recv, m_send, m_recv,
@@ -121,11 +121,18 @@
     inner = (z > 0) & (z < last)
     far_source = (2 - z) * last
     far_target = (z - 1) * last
+    middle_source = last - z
 
     def each_reach(act):
         for e in (2, -2, 1, -1):
             place = z + e
             pl.when((place >= 0) & (place <= last))(functools.partial(act, place))
+
+    def each_pixel_reach(act):
+        for e in (2, -2, 1, -1):
+            place = z + e
+            inside = (place >= 0) & (place <= last)
+            pl.when(inside if abs(e) == 1 else inside & jnp.logical_not(inner))(functools.partial(act, place))
 
     def each_source(act):
         for place in range(line_n):
@@ -197,23 +204,26 @@
     def x_arrival(s, place):
         return remote(x_part(s, place), x_part(s, place), x_send.at[s, place], x_recv.at[s, place], sibling)
 
-    def x_pass_on(s):
-        part = x_part(s, far_source)
-        return remote(part, part, x_send.at[s, z], x_recv.at[s, far_source], on_line(far_target))
+    def x_pass_on(s, source, sem):
+        part = x_part(s, source)
+        return remote(part, part, x_send.at[s, sem], x_recv.at[s, source], on_line(far_target))
 
     def pass_on_pixels(s):
         @pl.when(inner)
         def _():
+            x_arrival(s, middle_source).wait_recv()
+            x_pass_on(s, middle_source, far_source).start()
             x_arrival(s, far_source).wait_recv()
-            x_pass_on(s).start()
+            x_pass_on(s, far_source, z).start()
 
     for s in range(blocks):
-        each_reach(lambda place, s=s: x_copy(s, place).start())
+        each_pixel_reach(lambda place, s=s: x_copy(s, place).start())
         for copy in conv[s : s + 1]:
             copy.start()
     for copy in conv[blocks:]:
         copy.start()
     pass_on_pixels(0)
+    pass_on_pixels(1)
 
     forwards = []
     for d in range(1, tm_n):
@@ -228,9 +238,9 @@
         remote(part, part, conv_fwd_send.at[d - 1], conv_fwd_recv.at[d - 1], sibling).wait_recv()
     for copy in own_blocks:
         copy.wait()
+    pl.when(blocks > 2)(lambda: pass_on_pixels(2))
     kernel[...] = turned[...].T
     weights.wait()
-    pass_on_pixels(1)
 
     mine = pl.ds(pl.multiple_of(core * line_rows, line_rows), line_rows)
     other = pl.ds(pl.multiple_of((1 - core) * line_rows, line_rows), line_rows)
@@ -265,7 +275,8 @@
 
     def embed_block(s):
         def arrived(place):
-            pl.when(jnp.logical_not(inner & (far_source == place)))(lambda: x_arrival(s, place).wait_recv())
+            passed = inner & ((far_source == place) | (middle_source == place))
+            pl.when(jnp.logical_not(passed))(lambda: x_arrival(s, place).wait_recv())
 
         each_source(arrived)
         tail = xs[s, :, 4 * main :].astype(jnp.float32)
@@ -304,7 +315,7 @@
 
     def first_half(s, carry):
         pl.when(s < blocks)(lambda: embed_block(s))
-        pl.when(s + 2 < blocks)(lambda: pass_on_pixels(s + 2))
+        pl.when(s + 3 < blocks)(lambda: pass_on_pixels(s + 3))
         pl.when(s > 0)(lambda: hidden_block(s - 1))
         pl.when(s > 2)(lambda: pass_on_hidden(s - 3))
         return carry
@@ -328,18 +339,51 @@
         part = h_part(s, z * 2 + 1 - core)
         remote(part, part, h_own_send.at[s], h_own_recv.at[s], sibling).wait_recv()
         each_source(lambda place: h_across(s, place, 1 - core).wait_recv())
+        for n in range(0, out_ref.shape[1], 256):
+            product = jnp.dot(hidden[s], wout[:, n : n + 256], preferred_element_type=jnp.float32)
+            put_tokens(s, n, product + bias_out[:, n : n + 256])
+
+    def put_tokens(s, n, result):
         pair, band = s // bands, lax.rem(s, bands)
+        for c in range(2):
+            for l in range(line_n):
+                at = ((pair * tp_n + l * 2 + c) * bands + band) * cols
+                low = c * line_rows + l * (cols // 2)
+                high = low + line_rows // 2
+                tokens = [result[low : low + cols // 2], result[high : high + cols // 2]]
+                tokens = jnp.concatenate(tokens, axis=0).astype(jnp.bfloat16)
+                out_ref[pl.ds(pl.multiple_of(at, cols), cols), n : n + 256] = tokens
+
+    def last_block(s):
+        def take(place):
+            pl.when(jnp.logical_not(inner & (far_source == place)))(lambda: h_arrival(s, place).wait_recv())
+            h_across(s, place, core).start()
+
+        def add(place):
+            at = pl.multiple_of(place * 2 * hid_local, 128)
+            for n in range(0, out_ref.shape[1], 256):
+                part = jnp.dot(
+                    hidden[s, :, pl.ds(at, 2 * hid_local)],
+                    wout[pl.ds(at, 2 * hid_local), n : n + 256],
+                    preferred_element_type=jnp.float32,
+                )
+                total[:, n : n + 256] += part
+
+        upper = z // 2
+        order = (1 - z + 4 * upper, 2 - upper, 3 - 3 * upper)
+        total[...] = jnp.broadcast_to(bias_out, total.shape)
+        pass_on_hidden(s)
+        part = h_part(s, z * 2 + 1 - core)
+        remote(part, part, h_own_send.at[s], h_own_recv.at[s], sibling).wait_recv()
+        ready = z
+        for place in order:
+            take(place)
+            add(ready)
+            h_across(s, place, 1 - core).wait_recv()
+            ready = place
+        add(ready)
         for n in range(0, out_ref.shape[1], 256):
-            total = jnp.dot(hidden[s], wout[:, n : n + 256], preferred_element_type=jnp.float32)
-            result = total + bias_out[:, n : n + 256]
-            for c in range(2):
-                for l in range(line_n):
-                    at = ((pair * tp_n + l * 2 + c) * bands + band) * cols
-                    low = c * line_rows + l * (cols // 2)
-                    high = low + line_rows // 2
-                    tokens = [result[low : low + cols // 2], result[high : high + cols // 2]]
-                    tokens = jnp.concatenate(tokens, axis=0).astype(jnp.bfloat16)
-                    out_ref[pl.ds(pl.multiple_of(at, cols), cols), n : n + 256] = tokens
+            put_tokens(s, n, total[:, n : n + 256])
 
     hand_over(0)
 
@@ -348,8 +392,9 @@
         second_half(s - 1)
         return carry
 
-    lax.fori_loop(1, blocks, finish, 0)
-    second_half(blocks - 1)
+    lax.fori_loop(1, blocks - 1, finish, 0)
+    second_half(blocks - 2)
+    last_block(blocks - 1)
 
     for copy in conv + forwards:
         copy.wait_send()
@@ -357,13 +402,14 @@
     def drain(s, carry):
         remote(merged.at[s, mine], merged.at[s, mine], m_send.at[s], m_recv.at[s], sibling).wait_send()
         remote(h_part(s, tp), h_part(s, tp), h_own_send.at[s], h_own_recv.at[s], sibling).wait_send()
-        each_reach(lambda place: x_copy(s, place).wait_send())
+        each_pixel_reach(lambda place: x_copy(s, place).wait_send())
         each_reach(lambda place: h_copy(s, place).wait_send())
         each_source(lambda place: h_across(s, place, core).wait_send())
 
         @pl.when(inner)
         def _():
-            x_pass_on(s).wait_send()
+            x_pass_on(s, middle_source, far_source).wait_send()
+            x_pass_on(s, far_source, z).wait_send()
             h_pass_on(s).wait_send()
 
         return carry
@@ -404,6 +450,7 @@
             pltpu.VMEM((blocks, group, proj_out.shape[0]), bf16),
             pltpu.VMEM(proj_in.shape, bf16),
             pltpu.VMEM(proj_out.shape, bf16),
+            pltpu.VMEM((group, proj_out.shape[1]), jnp.float32),
             dma((1 + blocks,)),
             dma((2,)),
         ]
@@ -434,7 +481,7 @@
         and tm_n >= 2
         and tp_n % 2 == 0
         and tp_n == 8
-        and pairs * rows >= 4
+        and pairs * rows >= 6
         and local % 32 == 0
         and local * tm_n % 256 == 0
         and patch % 128 != 0

time: 99.3 us -> 98 us (0.987)
  Pallas kernels: 96.8 us -> 95.1 us
    pallas_call x1, Pallas kernels: 96.8 us -> 95.1 us  [per_device_fused(): pl.pallas_call(functools.partial(fused_kernel, (tm_n, tp_n, pairs, bands,...]
where the time goes in v7:
time: 98 us; the launch traced here: 97.5 us
  Pallas kernels  95.1 us (97%)
  local copies, waits for them, and re-layouts  2.31 us (2%)
    pallas_call x1, Pallas kernels, per_device_fused(): pl.pallas_call(functools.partial(fused_kernel, (tm_n, tp_n, pairs, bands,...  95.1 us
    unnamed x1, local copies, waits for them, and re-layouts  2.31 us

profile of v7, /device:TPU:0, one launch (start us, length us, event | category | flops | bytes accessed | tf_op | source)
XLA Modules:
  0.0 97.5 jit_solution(8831374166694400889)
XLA Ops:
  0.0 95.1 %shard_map.82 = bf16[512,1024]{1,0:T(8,128)(2,1)} custom-call(bf16[4,64,1176]{2,1,0:T(8,128)(2,1)} %bitcast.5, bf16[320,1176]{1,0:T(8,128)(2,1)} %bitcast.4, f32[1280]{0:T(1024)} %gain_ref.1, f32[1280]{0:T(1024)} %shift_ref.1, f32[640]{0:T(1024)} %bias_in_ref.1, f32[1024]{0:T(1024)} %bias_out_ref.1, bf16[5120,640]{1,0:T(8,128)(2,1)} %proj_in_ref.1, ...), custom_call_target="tpu_custom_call" | custom-call | tf_op jit(solution)/shard_map/pallas_call | solution.py:437
  95.2 2.3 %copy.10 = bf16[2,16,16,1024]{3,2,1,0:T(8,128)(2,1)} copy(bf16[2,16,16,1024]{3,2,1,0:T(8,128)(2,1)} %bitcast.3) | data formatting | bytes 2097152
